TPU v7x, 32 devices: a whole 2x2x4 slice. The times are simulated.
32 devices in a mesh: chan: 16 (over z, y, core), tm: 2 (over x).
Axes of the slice: x: 2, y: 2, z: 4, core: 2. Of those that a mesh axis runs over, the one named last changes fastest.
Arguments:
- samples: bfloat16 [256, 4096], P('chan', 'tm'), may hold values from -6 to 6
- fir_taps: float32 [96], replicated, may hold values from -0.625 to 0.625
- plan: int32 [4], replicated, may hold values from 1 to 15, as said below
Outputs:
- self_corr: float32 [256, 16, 129], P(('chan', 'tm'))
- pair_corr: float32 [4, 256, 16, 129], P(None, ('chan', 'tm'))
Inputs may be any that keep to these rules, and one draw needn't show every extreme that they name: Round r pairs block g with block g XOR plan[r]; the masks of the rounds are distinct, and the values 1 and 15 both occur.
All inputs are finite; a program needn't handle non-finite values.
Results may differ from a plain program's by a relative error of at most 0.0043.
Values may be sent and summed in bfloat16 or wider, within the bound.
No kernel may reach another device: no remote copies, remote signals or barrier semaphores. Data moves between devices by JAX's collectives and lax.ppermute only.
A program may use at most 128 MiB of HBM per device.

v0:
```python
import functools
import math

import jax
import jax.numpy as jnp
import ml_dtypes
import numpy as np
from jax import lax
from jax.experimental import pallas as pl
from jax.experimental.pallas import tpu as pltpu
from jax.sharding import PartitionSpec as P

SEGS_DEV = 2
LAGS = 129
ROUNDS = 4
LANE = 128
MAX_BRANCHES = 128
OUT_GROUPS = 2
VMEM_LIMIT = 8 * 1024 * 1024
KERNEL_VMEM = 24 * 1024 * 1024
VMEM = pl.BlockSpec(memory_space=pltpu.VMEM)
SMEM = pl.BlockSpec(memory_space=pltpu.SMEM)
HBM = pl.BlockSpec(memory_space=pl.ANY)


def split_table(table):
    high = table.astype(ml_dtypes.bfloat16)
    low = (table - high.astype(np.float64)).astype(ml_dtypes.bfloat16)
    return np.concatenate([high, high, low], axis=0)


def tables(length):
    half = length // 2
    quarter = length // 4
    sample = np.arange(half)[:, None]

    def columns(freqs):
        angle = 2.0 * math.pi / length * (sample * freqs[None, :] % length)
        return np.cos(angle), -np.sin(angle)

    even = 2 * np.arange(quarter)
    odd = even + 1
    even_re, even_im = columns(even)
    even_im[:, 0] = 1.0 - 2.0 * (np.arange(half) % 2)
    odd_re, odd_im = columns(odd)
    even_table = np.concatenate([even_re, even_im], axis=1)
    odd_table = np.concatenate([odd_re, odd_im], axis=1)

    freqs = np.concatenate([even, odd])[:, None]
    lag = (np.arange(LAGS) - LAGS // 2)[None, :]
    angle = 2.0 * math.pi / length * (lag * freqs % length)
    weight = np.where(freqs == 0, 1.0, 2.0) / length
    lag_cos = weight * np.cos(angle)
    lag_sin = weight * np.sin(angle)
    lag_sin[0] = (1.0 - 2.0 * (np.abs(lag[0]) % 2)) / length
    lag_table = np.zeros((length, 2 * LANE))
    lag_table[:, :LAGS] = np.concatenate([lag_cos, lag_sin], axis=0)
    return (
        split_table(even_table),
        split_table(odd_table),
        lag_table.astype(ml_dtypes.bfloat16),
    )


def dot(left, right):
    return jnp.dot(left, right, preferred_element_type=jnp.float32)


def free_masks_of(plan, last_mask):
    masks = [plan[r] for r in range(ROUNDS)]
    free = [(mask != 1) & (mask != last_mask) for mask in masks]
    low = functools.reduce(
        jnp.minimum, [jnp.where(ok, mask, last_mask) for ok, mask in zip(free, masks)]
    )
    high = functools.reduce(jnp.maximum, [jnp.where(ok, mask, 0) for ok, mask in zip(free, masks)])
    return low, high


def prepare_kernel(last_mask, plan, taps, samples, *refs):
    tables_hbm, (branch, record, toep), refs = refs[:2], refs[2:5], refs[5:]
    tables_vmem, (own_sem, table_sems) = refs[:2], refs[2:]
    chans = samples.shape[0]
    copies = [pltpu.make_async_copy(samples, record.at[pl.ds(0, chans)], own_sem)]
    copies += [
        pltpu.make_async_copy(table, table_vmem, table_sems.at[i])
        for i, (table, table_vmem) in enumerate(zip(tables_hbm, tables_vmem))
    ]
    for copy in copies:
        copy.start()
    low, high = (mask - 2 for mask in free_masks_of(plan, last_mask))
    branch[0] = high * (high - 1) // 2 + low

    lane = lax.broadcasted_iota(jnp.int32, (1, 2 * LANE), 1)
    base = jnp.zeros((1, 2 * LANE), jnp.float32)
    for j in range(taps.shape[0]):
        base = jnp.where(lane == j, taps[j], base)
    base = jnp.broadcast_to(base, (2 * LANE, 2 * LANE))
    toeplitz = pltpu.roll(base, LANE, 1, stride=1, stride_axis=0)[:, :LANE]
    toep_hi = toeplitz.astype(jnp.bfloat16)
    toep[:, :LANE] = toep_hi
    toep[:, LANE:] = (toeplitz - toep_hi.astype(jnp.float32)).astype(jnp.bfloat16)
    for copy in copies:
        copy.wait()


def prepare(plan, fir_taps, samples, last_mask, parts):
    chans, width = samples.shape
    *table_list, lag_table = tables(width // SEGS_DEV)
    plan, fir_taps, samples, *table_list = (
        pltpu.with_memory_space_constraint(jnp.asarray(array), pltpu.HBM)
        for array in (plan, fir_taps, samples, *table_list)
    )
    branch, record, toep, *table_list = pl.pallas_call(
        functools.partial(prepare_kernel, last_mask),
        out_shape=(
            jax.ShapeDtypeStruct((1,), jnp.int32),
            pltpu.VMEM((parts * chans, width), jnp.bfloat16),
            pltpu.VMEM((2 * LANE, 2 * LANE), jnp.bfloat16),
            *[pltpu.VMEM(table.shape, jnp.bfloat16) for table in table_list],
        ),
        in_specs=[SMEM, SMEM] + [HBM] * (1 + len(table_list)),
        out_specs=(SMEM,) + (VMEM,) * (2 + len(table_list)),
        scratch_shapes=[
            pltpu.SemaphoreType.DMA,
            pltpu.SemaphoreType.DMA((len(table_list),)),
        ],
        compiler_params=pltpu.CompilerParams(vmem_limit_bytes=VMEM_LIMIT),
    )(plan, fir_taps, samples, *table_list)
    return branch, record, (toep, *table_list, jnp.asarray(lag_table))


def add_spectra(columns_of, place, parts, shape, first_row, refs):
    chans, width = shape
    toep, sums, diffs = refs
    half = width // SEGS_DEV // 2
    tiles = half // LANE
    for piece in range(parts):
        tail = columns_of((piece + 1) % parts, width - LANE, width)
        has_before = jnp.where(lax.rem(place + parts - piece, parts) == 0, 0.0, 1.0)
        tail = (tail.astype(jnp.float32) * has_before).astype(jnp.bfloat16)
        windows = [jnp.concatenate([tail, columns_of(piece, 0, LANE)], axis=1)]
        windows += [
            columns_of(piece, LANE * (k - 1), LANE * (k + 1)) for k in range(1, width // LANE)
        ]
        both = dot(jnp.concatenate(windows, axis=0), toep[...])
        filtered = both[:, :LANE] + both[:, LANE:]
        for s in range(SEGS_DEV):
            row = first_row + (piece * SEGS_DEV + s) * chans
            for k in range(tiles):
                lo = (s * 2 * tiles + k) * chans
                hi = lo + tiles * chans
                first, second = filtered[lo : lo + chans], filtered[hi : hi + chans]
                for ref, value in ((sums, first + second), (diffs, first - second)):
                    high = value.astype(jnp.bfloat16)
                    low = (value - high.astype(jnp.float32)).astype(jnp.bfloat16)
                    for j, part in enumerate((high, low, high)):
                        at = half * j + LANE * k
                        ref[row : row + chans, at : at + LANE] = part


def whiten(sums, diffs, even_table, odd_table, real_ref, imag_ref):
    half = even_table.shape[1]
    quarter = half // 2
    even = dot(sums[...], even_table[...])
    odd = dot(diffs[...], odd_table[...])
    real = jnp.concatenate([even[:, :quarter], odd[:, :quarter]], axis=1)
    imag = jnp.concatenate([even[:, quarter:], odd[:, quarter:]], axis=1)
    edge = lax.broadcasted_iota(jnp.int32, real.shape, 1) == 0
    real_sq = real * real
    imag_sq = imag * imag
    level = 0.1 / (half + 1) * jnp.sum(real_sq + imag_sq, axis=1, keepdims=True) + 1e-06
    inv_real = lax.rsqrt(real_sq + jnp.where(edge, 0.0, imag_sq) + level)
    inv_imag = jnp.where(edge, lax.rsqrt(imag_sq + level), inv_real)
    real_ref[...] = (real * inv_real).astype(jnp.bfloat16).astype(jnp.float32)
    imag_ref[...] = (imag * inv_imag).astype(jnp.bfloat16).astype(jnp.float32)


def cross_spectra(first, count, chans, segs, left_ref, real_ref, imag_ref, cross):
    rows, half = real_ref.shape
    rows_blk = segs * chans
    sets = rows // rows_blk

    @pl.loop(0, count)
    def _(i):
        a = first + i
        at = pl.multiple_of(a * sets * chans, sets * chans)
        for c in range(half // LANE):
            cols = slice(LANE * c, LANE * (c + 1))
            left = [
                jnp.broadcast_to(left_ref[a, j : j + 1, cols], (chans, LANE))
                for j in range(3 * segs)
            ]
            for q in range(sets):
                cos_part = sin_part = 0.0
                for s in range(segs):
                    row_b = slice(q * rows_blk + s * chans, q * rows_blk + (s + 1) * chans)
                    re_b, im_b = real_ref[row_b, cols], imag_ref[row_b, cols]
                    re_a, im_a, x_a = (left[segs * j + s] for j in range(3))
                    cos_part += re_a * re_b + im_a * im_b
                    sin_part += x_a * im_b - im_a * re_b
                at_q = pl.ds(at + q * chans, chans)
                cross[at_q, cols] = cos_part.astype(jnp.bfloat16)
                cross[at_q, half + LANE * c : half + LANE * (c + 1)] = sin_part.astype(jnp.bfloat16)


def spectra_scratch(sets, parts, chans, length, share):
    rows, half = sets * parts * SEGS_DEV * chans, length // 2
    return [
        pltpu.VMEM((rows, 3 * half), jnp.bfloat16),
        pltpu.VMEM((rows, 3 * half), jnp.bfloat16),
        pltpu.VMEM((rows, half), jnp.float32),
        pltpu.VMEM((rows, half), jnp.float32),
        pltpu.VMEM((share * sets * chans, length), jnp.bfloat16),
    ]


def rows_of_block(block, chans):
    return lambda piece, lo, hi: block[piece * chans : (piece + 1) * chans, lo:hi]


def correlate_kernel(parts, last_mask, plan, toep, even_table, odd_table, lag_hbm, *refs):
    own, far, near, low, high, refs = *refs[:5], refs[5:]
    far_more, (self_out, pair_out), refs = refs[: parts - 1], refs[parts - 1 : parts + 1], refs[parts + 1 :]
    lag_table, arrived, far_arrived, left_ref, sums, diffs, real_ref, imag_ref, cross, staged = refs[:10]
    lag_sem, sems, far_sems, out_sems = refs[10:]

    chans, width = far.shape
    half = even_table.shape[1]
    share = left_ref.shape[0]
    segs = parts * SEGS_DEV
    sets = ROUNDS + 1
    place = lax.axis_index("tm")
    copies = [
        pltpu.make_async_copy(source, arrived.at[i], sems.at[i])
        for i, source in enumerate((near, low, high))
    ]
    far_copies = [
        pltpu.make_async_copy(source, far_arrived.at[i], far_sems.at[i])
        for i, source in enumerate(far_more)
    ]
    lag_copy = pltpu.make_async_copy(lag_hbm, lag_table, lag_sem)
    for copy in far_copies + copies + [lag_copy]:
        copy.start()

    def far_columns(piece, lo, hi):
        return far[:, lo:hi] if piece == 0 else far_arrived[piece - 1, :, lo:hi]

    blocks = [
        (rows_of_block(own, chans), []),
        (rows_of_block(arrived.at[0], chans), copies[:1]),
        (far_columns, far_copies),
        (rows_of_block(arrived.at[1], chans), copies[1:2]),
        (rows_of_block(arrived.at[2], chans), copies[2:]),
    ]
    for q in (0, 2, 1, 3, 4):
        columns_of, needs = blocks[q]
        for copy in needs:
            copy.wait()
        first_row = q * segs * chans
        add_spectra(columns_of, place, parts, far.shape, first_row, (toep, sums, diffs))
    whiten(sums, diffs, even_table, odd_table, real_ref, imag_ref)

    def picked(ref, s):
        value = ref[s * chans : s * chans + share, :]
        for owner in range(1, parts):
            at = s * chans + owner * share
            value = jnp.where(place == owner, ref[at : at + share, :], value)
        return value

    edge = lax.broadcasted_iota(jnp.int32, (share, half), 1) == 0
    for s in range(segs):
        real_s, imag_s = picked(real_ref, s), picked(imag_ref, s)
        lefts = (real_s, jnp.where(edge, 0.0, imag_s), jnp.where(edge, imag_s, real_s))
        for j, value in enumerate(lefts):
            for a in range(share):
                left_ref[a, segs * j + s : segs * j + s + 1, :] = value[a : a + 1]

    low_mask, high_mask = free_masks_of(plan, last_mask)
    slots = [
        sum(jnp.where(plan[r] == mask, r, 0) for r in range(ROUNDS))
        for mask in (1, last_mask, low_mask, high_mask)
    ]
    outs = [self_out, *(pair_out.at[slot] for slot in slots)]
    lag_copy.wait()
    out_copies = []
    groups = OUT_GROUPS if share % OUT_GROUPS == 0 else 1
    count = share // groups
    for group in range(groups):
        first = group * count
        cross_spectra(first, count, chans, segs, left_ref, real_ref, imag_ref, cross)
        rows = slice(first * sets * chans, (first + count) * sets * chans)
        result = dot(cross[rows, :], lag_table[...])
        for i in range(count):
            for q in range(sets):
                at = (i * sets + q) * chans
                staged[q, first + i] = result[at : at + chans, :LAGS]
        for q, out in enumerate(outs):
            piece = pl.ds(first, count)
            sem = out_sems.at[group * sets + q]
            out_copies.append(pltpu.make_async_copy(staged.at[q, piece], out.at[piece], sem))
            out_copies[-1].start()
    for copy in out_copies:
        copy.wait()


def correlate(plan, table_list, own, near, far, far_more, low, high, last_mask):
    chans, width = far.shape
    parts = len(far_more) + 1
    share = chans // parts
    length = width // SEGS_DEV
    sets = ROUNDS + 1
    *table_list, lag_table = table_list
    plan, lag_table = (
        pltpu.with_memory_space_constraint(array, pltpu.HBM) for array in (plan, lag_table)
    )
    return pl.pallas_call(
        functools.partial(correlate_kernel, parts, last_mask),
        out_shape=(
            jax.ShapeDtypeStruct((share, chans, LAGS), jnp.float32),
            jax.ShapeDtypeStruct((ROUNDS, share, chans, LAGS), jnp.float32),
        ),
        in_specs=[SMEM] + [VMEM] * len(table_list) + [HBM] + [VMEM] * 2 + [HBM] * (parts + 2),
        out_specs=(HBM, HBM),
        scratch_shapes=[
            pltpu.VMEM(lag_table.shape, jnp.bfloat16),
            pltpu.VMEM((3, *own.shape), jnp.bfloat16),
            pltpu.VMEM((parts - 1, chans, width), jnp.bfloat16),
            pltpu.VMEM((share, 3 * parts * SEGS_DEV, length // 2), jnp.float32),
            *spectra_scratch(sets, parts, chans, length, share),
            pltpu.VMEM((sets, share, chans, LAGS), jnp.float32),
            pltpu.SemaphoreType.DMA,
            pltpu.SemaphoreType.DMA((3,)),
            pltpu.SemaphoreType.DMA((parts - 1,)),
            pltpu.SemaphoreType.DMA((sets * OUT_GROUPS,)),
        ],
        compiler_params=pltpu.CompilerParams(vmem_limit_bytes=KERNEL_VMEM),
    )(plan, *table_list, lag_table, own, far, near, low, high, *far_more)


def from_partner(block, mask):
    chan_count = lax.axis_size("chan")
    return lax.ppermute(block, "chan", [(g, g ^ mask) for g in range(chan_count)])


def from_times(block):
    parts = lax.axis_size("tm")
    return [
        lax.ppermute(block, "tm", [(t, (t + j) % parts) for t in range(parts)])
        for j in range(1, parts)
    ]


def on_device(samples, fir_taps, plan):
    chan_count, parts = lax.axis_size("chan"), lax.axis_size("tm")
    chans = samples.shape[0]
    near_mask, far_mask = 1, chan_count - 1
    free_masks = range(2, far_mask)

    far = from_partner(samples, far_mask)
    others = from_times(samples)
    branch, own, table_list = prepare(plan, fir_taps, samples, far_mask, parts)
    for j, piece in enumerate(others):
        own = lax.dynamic_update_slice(own, piece, ((j + 1) * chans, 0))

    def send(masks, far, own):
        return from_partner(own, near_mask), from_times(far), *[from_partner(own, m) for m in masks]

    pairs = [(low, high) for high in free_masks for low in free_masks if low < high]
    if len(pairs) <= MAX_BRANCHES:
        branches = [functools.partial(send, pair) for pair in pairs]
        near, far_more, low, high = lax.switch(branch.reshape(()), branches, far, own)
    else:
        sends = [functools.partial(from_partner, mask=mask) for mask in free_masks]
        low, high = (
            lax.switch(mask - free_masks[0], sends, own) for mask in free_masks_of(plan, far_mask)
        )
        near, far_more = send((), far, own)
    return correlate(plan, table_list, own, near, far, far_more, low, high, far_mask)


def solution(mesh):
    in_specs = (P("chan", "tm"), P(), P())
    out_specs = (P(("chan", "tm"), None, None), P(None, ("chan", "tm"), None, None))
    return jax.shard_map(
        on_device, mesh=mesh, in_specs=in_specs, out_specs=out_specs, check_vma=False
    )
```

profile of v0, /device:TPU:0, one launch (start us, length us, event | category | flops | bytes accessed | tf_op | source)
XLA Modules:
  0.0 28.4 jit_solution(12556618605033667522)
XLA Ops:
  0.6 3.0 %collective-permute-start.312 = (bf16[16,2048]{1,0:T(8,128)(2,1)}, bf16[16,2048]{1,0:T(8,128)(2,1)S(1)}, u32[]{:S(2)}, u32[]{:S(2)}) collective-permute-start(bf16[16,2048]{1,0:T(8,128)(2,1)} %samples.1), channel_id=1, source_target_pairs={{0,1},{1,0},{2,3},{3,2},{4,5},{5,4},{6,7},{7,6},{8,9},{9,8},{10,11... | collective-permute-start | bytes 196616 | tf_op jit(solution)/shard_map/ppermute | solution.py:348
  3.6 3.7 %collective-permute-start.313 = (bf16[16,2048]{1,0:T(8,128)(2,1)}, bf16[16,2048]{1,0:T(8,128)(2,1)S(1)}, u32[]{:S(2)}, u32[]{:S(2)}) collective-permute-start(bf16[16,2048]{1,0:T(8,128)(2,1)} %samples.1), channel_id=1, source_target_pairs={{0,30},{2,28},{4,26},{6,24},{8,22},{10,20},{12,18},{14,16},{16,14}... | collective-permute-start | bytes 196616 | tf_op jit(solution)/shard_map/ppermute | solution.py:342
  7.4 3.2 %shard_map.77 = (s32[1]{0:T(128)}, bf16[32,2048]{1,0:T(8,128)(2,1)S(1)}, bf16[256,256]{1,0:T(8,128)(2,1)S(1)}, bf16[1536,512]{1,0:T(8,128)(2,1)S(1)}, bf16[1536,512]{1,0:T(8,128)(2,1)S(1)}) custom-call(s32[4]{0:T(128)} %plan.3, f32[96]{0:T(128)} %taps.1, bf16[16,2048]{1,0:T(8,128)(2,1)} %samples.1, bf16[1536,512]{1,0:T(8,128)(2,1)} %constant.15.clone.refs_0_, ...), custom_call_target="tpu_custom_call" | custom-call | tf_op jit(solution)/shard_map/pallas_call | solution.py:113
  11.2 0.0 collective-permute-done.312
  11.2 0.0 collective-permute-done.313.refs_1_
  11.2 9.6 %conditional.1 = (bf16[32,2048]{1,0:T(8,128)(2,1)}, bf16[16,2048]{1,0:T(8,128)(2,1)}, bf16[32,2048]{1,0:T(8,128)(2,1)}, bf16[32,2048]{1,0:T(8,128)(2,1)}) conditional(s32[]{:T(128)} %bitcast, (bf16[32,2048]{1,0:T(8,128)(2,1)S(1)}, bf16[16,2048]{1,0:T(8,128)(2,1)S(1)}) %tuple.319, (bf16[32,2048]{1,0:T(8,128)(2,1)S(1)}, ...), branch_computations={%region_0.0_spmd, %region_1.0_spmd, %region_2.0_spmd, %region_3.0_... | conditional | bytes 1835200 | solution.py:371
  11.2 0.1 collective-permute-start.91
  11.3 1.4 %collective-permute-start.90 = (bf16[32,2048]{1,0:T(8,128)(2,1)S(1)}, bf16[32,2048]{1,0:T(8,128)(2,1)}, u32[]{:S(2)}, u32[]{:S(2)}) collective-permute-start(bf16[32,2048]{1,0:T(8,128)(2,1)S(1)} %get-tuple-element.356), channel_id=1, source_target_pairs={{0,6},{2,4},{4,2},{6,0},{8,14},{10,12},{12,10},{14,8},{16,22},{18,... | collective-permute-start | bytes 393224 | tf_op jit(solution)/shard_map/cond/branch_22_fun/ppermute | solution.py:342
  12.7 0.0 collective-permute-start.88
  12.7 0.5 %collective-permute-start.89 = (bf16[16,2048]{1,0:T(8,128)(2,1)S(1)}, bf16[16,2048]{1,0:T(8,128)(2,1)}, u32[]{:S(2)}, u32[]{:S(2)}) collective-permute-start(bf16[16,2048]{1,0:T(8,128)(2,1)S(1)} %get-tuple-element.357), channel_id=1, source_target_pairs={{0,1},{1,0},{2,3},{3,2},{4,5},{5,4},{6,7},{7,6},{8,9},{9,8},{10,11... | collective-permute-start | bytes 196616 | tf_op jit(solution)/shard_map/cond/branch_22_fun/ppermute | solution.py:348
  13.2 4.1 %collective-permute-done.89 = bf16[16,2048]{1,0:T(8,128)(2,1)} collective-permute-done((bf16[16,2048]{1,0:T(8,128)(2,1)S(1)}, bf16[16,2048]{1,0:T(8,128)(2,1)}, u32[]{:S(2)}, u32[]{:S(2)}) %collective-permute-start.89) | collective-permute-done | bytes 65568 | tf_op jit(solution)/shard_map/cond/branch_22_fun/ppermute | solution.py:348
  17.3 3.5 %collective-permute-done.91 = bf16[32,2048]{1,0:T(8,128)(2,1)} collective-permute-done((bf16[32,2048]{1,0:T(8,128)(2,1)S(1)}, bf16[32,2048]{1,0:T(8,128)(2,1)}, u32[]{:S(2)}, u32[]{:S(2)}) %collective-permute-start.91) | collective-permute-done | bytes 131104 | tf_op jit(solution)/shard_map/cond/branch_22_fun/ppermute | solution.py:342
  20.8 0.0 collective-permute-done.90
  20.8 0.0 collective-permute-done.88
  20.8 7.4 %shard_map.78 = (f32[8,16,129]{2,1,0:T(8,128)}, f32[4,8,16,129]{3,2,1,0:T(8,128)}) custom-call(s32[4]{0:T(128)} %plan.3, bf16[256,256]{1,0:T(8,128)(2,1)S(1)} %get-tuple-element.479.toep, bf16[1536,512]{1,0:T(8,128)(2,1)S(1)} %get-tuple-element.480.even_table, bf16[1536,512]{1,0:T(8,128)(2,1)S(1)} %get-tuple-element.481.odd_table, ...), custom_call_target="tpu_custom_call" | custom-call | tf_op jit(solution)/shard_map/pallas_call | solution.py:316
  (1 shorter events, 0.0 us)
Async XLA Ops:
  0.6 10.5 %collective-permute-start.312 = (bf16[16,2048]{1,0:T(8,128)(2,1)}, bf16[16,2048]{1,0:T(8,128)(2,1)S(1)}, u32[]{:S(2)}, u32[]{:S(2)}) collective-permute-start(bf16[16,2048]{1,0:T(8,128)(2,1)} %samples.1), channel_id=1, source_target_pairs={{0,1},{1,0},{2,3},{3,2},{4,5},{5,4},{6,7},{7,6},{8,9},{9,8},{10,11... | collective-permute-start | bytes 196616 | tf_op jit(solution)/shard_map/ppermute | solution.py:348
  3.6 7.6 %collective-permute-start.313 = (bf16[16,2048]{1,0:T(8,128)(2,1)}, bf16[16,2048]{1,0:T(8,128)(2,1)S(1)}, u32[]{:S(2)}, u32[]{:S(2)}) collective-permute-start(bf16[16,2048]{1,0:T(8,128)(2,1)} %samples.1), channel_id=1, source_target_pairs={{0,30},{2,28},{4,26},{6,24},{8,22},{10,20},{12,18},{14,16},{16,14}... | collective-permute-start | bytes 196616 | tf_op jit(solution)/shard_map/ppermute | solution.py:342
  11.2 9.5 %collective-permute-start.91 = (bf16[32,2048]{1,0:T(8,128)(2,1)S(1)}, bf16[32,2048]{1,0:T(8,128)(2,1)}, u32[]{:S(2)}, u32[]{:S(2)}) collective-permute-start(bf16[32,2048]{1,0:T(8,128)(2,1)S(1)} %get-tuple-element.356), channel_id=1, source_target_pairs={{0,18},{2,16},{4,22},{6,20},{8,26},{10,24},{12,30},{14,28},{16,2},... | collective-permute-start | bytes 393224 | tf_op jit(solution)/shard_map/cond/branch_22_fun/ppermute | solution.py:342
  11.3 9.5 %collective-permute-start.90 = (bf16[32,2048]{1,0:T(8,128)(2,1)S(1)}, bf16[32,2048]{1,0:T(8,128)(2,1)}, u32[]{:S(2)}, u32[]{:S(2)}) collective-permute-start(bf16[32,2048]{1,0:T(8,128)(2,1)S(1)} %get-tuple-element.356), channel_id=1, source_target_pairs={{0,6},{2,4},{4,2},{6,0},{8,14},{10,12},{12,10},{14,8},{16,22},{18,... | collective-permute-start | bytes 393224 | tf_op jit(solution)/shard_map/cond/branch_22_fun/ppermute | solution.py:342
  12.7 8.1 %collective-permute-start.88 = (bf16[32,2048]{1,0:T(8,128)(2,1)S(1)}, bf16[32,2048]{1,0:T(8,128)(2,1)}, u32[]{:S(2)}, u32[]{:S(2)}) collective-permute-start(bf16[32,2048]{1,0:T(8,128)(2,1)S(1)} %get-tuple-element.356), channel_id=1, source_target_pairs={{0,2},{2,0},{4,6},{6,4},{8,10},{10,8},{12,14},{14,12},{16,18},{18,... | collective-permute-start | bytes 393224 | tf_op jit(solution)/shard_map/cond/branch_22_fun/ppermute | solution.py:342
  12.7 4.6 %collective-permute-start.89 = (bf16[16,2048]{1,0:T(8,128)(2,1)S(1)}, bf16[16,2048]{1,0:T(8,128)(2,1)}, u32[]{:S(2)}, u32[]{:S(2)}) collective-permute-start(bf16[16,2048]{1,0:T(8,128)(2,1)S(1)} %get-tuple-element.357), channel_id=1, source_target_pairs={{0,1},{1,0},{2,3},{3,2},{4,5},{5,4},{6,7},{7,6},{8,9},{9,8},{10,11... | collective-permute-start | bytes 196616 | tf_op jit(solution)/shard_map/cond/branch_22_fun/ppermute | solution.py:348
where the time goes:
time: 28.5 us; the launch traced here: 28.4 us
  Pallas kernels  10.6 us (37%)
  starting transfers between devices  8.71 us (31%)
  waiting for transfers between devices  7.56 us (27%)
  between operations  1.5 us (5%)
    pallas_call x1, Pallas kernels, correlate(): pl.pallas_call(functools.partial(correlate_kernel, parts, last_mask), out...  7.4 us
    ppermute x4, starting transfers between devices, from_partner(): lax.ppermute(block, 'chan', [(g, g ^ mask) for g in range(chan_count)])  5.17 us
    ppermute x2, waiting for transfers between devices, from_times(): lax.ppermute(block, 'tm', [(t, (t + j) % parts) for t in range(parts)])  4.08 us
    ppermute x2, starting transfers between devices, from_times(): lax.ppermute(block, 'tm', [(t, (t + j) % parts) for t in range(parts)])  3.54 us
    ppermute x4, waiting for transfers between devices, from_partner(): lax.ppermute(block, 'chan', [(g, g ^ mask) for g in range(chan_count)])  3.48 us
    pallas_call x1, Pallas kernels, prepare(): pl.pallas_call(functools.partial(prepare_kernel, last_mask), out_shape=(j...  3.16 us
  transfers between devices with their start and end apart: 6, of which 2 were waited for; matrix products, arithmetic and copies ran while one was open for 0% of the time, Pallas kernels for 11%

commit v1 on v0

--- a/solution.py
+++ b/solution.py
@@ -15,7 +15,7 @@
 ROUNDS = 4
 LANE = 128
 MAX_BRANCHES = 128
-OUT_GROUPS = 2
+OUT_GROUPS = 4
 VMEM_LIMIT = 8 * 1024 * 1024
 KERNEL_VMEM = 24 * 1024 * 1024
 VMEM = pl.BlockSpec(memory_space=pltpu.VMEM)
@@ -30,23 +30,19 @@
 
 
 def tables(length):
-    half = length // 2
     quarter = length // 4
-    sample = np.arange(half)[:, None]
-
-    def columns(freqs):
-        angle = 2.0 * math.pi / length * (sample * freqs[None, :] % length)
-        return np.cos(angle), -np.sin(angle)
-
-    even = 2 * np.arange(quarter)
-    odd = even + 1
-    even_re, even_im = columns(even)
-    even_im[:, 0] = 1.0 - 2.0 * (np.arange(half) % 2)
-    odd_re, odd_im = columns(odd)
-    even_table = np.concatenate([even_re, even_im], axis=1)
-    odd_table = np.concatenate([odd_re, odd_im], axis=1)
-
-    freqs = np.concatenate([even, odd])[:, None]
+
+    def packed(freqs, count):
+        angle = 2.0 * math.pi / length * (np.arange(count)[:, None] * freqs[None, :] % length)
+        return np.concatenate([np.cos(angle), -np.sin(angle)], axis=1)
+
+    fours = 4 * np.arange(quarter // 2)
+    odds = 2 * np.arange(quarter) + 1
+    sum_table = packed(fours, quarter)
+    sum_table[:, quarter // 2] = 1.0 - 2.0 * (np.arange(quarter) % 2)
+    fold_tables = sum_table, packed(fours + 2, quarter), packed(odds, 2 * quarter)
+
+    freqs = np.concatenate([fours, fours + 2, odds])[:, None]
     lag = (np.arange(LAGS) - LAGS // 2)[None, :]
     angle = 2.0 * math.pi / length * (lag * freqs % length)
     weight = np.where(freqs == 0, 1.0, 2.0) / length
@@ -55,11 +51,7 @@
     lag_sin[0] = (1.0 - 2.0 * (np.abs(lag[0]) % 2)) / length
     lag_table = np.zeros((length, 2 * LANE))
     lag_table[:, :LAGS] = np.concatenate([lag_cos, lag_sin], axis=0)
-    return (
-        split_table(even_table),
-        split_table(odd_table),
-        lag_table.astype(ml_dtypes.bfloat16),
-    )
+    return (*map(split_table, fold_tables), lag_table.astype(ml_dtypes.bfloat16))
 
 
 def dot(left, right):
@@ -77,8 +69,8 @@
 
 
 def prepare_kernel(last_mask, plan, taps, samples, *refs):
-    tables_hbm, (branch, record, toep), refs = refs[:2], refs[2:5], refs[5:]
-    tables_vmem, (own_sem, table_sems) = refs[:2], refs[2:]
+    tables_hbm, (branch, record, toep), refs = refs[:3], refs[3:6], refs[6:]
+    tables_vmem, (own_sem, table_sems) = refs[:3], refs[3:]
     chans = samples.shape[0]
     copies = [pltpu.make_async_copy(samples, record.at[pl.ds(0, chans)], own_sem)]
     copies += [
@@ -129,11 +121,10 @@
     return branch, record, (toep, *table_list, jnp.asarray(lag_table))
 
 
-def add_spectra(columns_of, place, parts, shape, first_row, refs):
+def add_spectra(columns_of, place, parts, shape, first_row, toep, folds):
     chans, width = shape
-    toep, sums, diffs = refs
-    half = width // SEGS_DEV // 2
-    tiles = half // LANE
+    tiles = width // SEGS_DEV // LANE
+    quarter = tiles // 4
     for piece in range(parts):
         tail = columns_of((piece + 1) % parts, width - LANE, width)
         has_before = jnp.where(lax.rem(place + parts - piece, parts) == 0, 0.0, 1.0)
@@ -146,33 +137,46 @@
         filtered = both[:, :LANE] + both[:, LANE:]
         for s in range(SEGS_DEV):
             row = first_row + (piece * SEGS_DEV + s) * chans
-            for k in range(tiles):
-                lo = (s * 2 * tiles + k) * chans
-                hi = lo + tiles * chans
-                first, second = filtered[lo : lo + chans], filtered[hi : hi + chans]
-                for ref, value in ((sums, first + second), (diffs, first - second)):
+            for k in range(quarter):
+                at = [(s * tiles + j * quarter + k) * chans for j in range(4)]
+                x = [filtered[lo : lo + chans] for lo in at]
+                even, later = x[0] + x[2], x[1] + x[3]
+                sums, diffs, odds = folds
+                for ref, tile, value in (
+                    (sums, k, even + later),
+                    (diffs, k, even - later),
+                    (odds, k, x[0] - x[2]),
+                    (odds, k + quarter, x[1] - x[3]),
+                ):
                     high = value.astype(jnp.bfloat16)
                     low = (value - high.astype(jnp.float32)).astype(jnp.bfloat16)
                     for j, part in enumerate((high, low, high)):
-                        at = half * j + LANE * k
+                        at = ref.shape[1] // 3 * j + LANE * tile
                         ref[row : row + chans, at : at + LANE] = part
 
 
-def whiten(sums, diffs, even_table, odd_table, real_ref, imag_ref):
-    half = even_table.shape[1]
-    quarter = half // 2
-    even = dot(sums[...], even_table[...])
-    odd = dot(diffs[...], odd_table[...])
-    real = jnp.concatenate([even[:, :quarter], odd[:, :quarter]], axis=1)
-    imag = jnp.concatenate([even[:, quarter:], odd[:, quarter:]], axis=1)
-    edge = lax.broadcasted_iota(jnp.int32, real.shape, 1) == 0
+def whiten(folds, fold_tables, real_ref, imag_ref):
+    products = [dot(fold[...], table[...]) for fold, table in zip(folds, fold_tables)]
+    real, imag = (
+        jnp.concatenate(
+            [p[:, p.shape[1] // 2 * j : p.shape[1] // 2 * (j + 1)] for p in products], axis=1
+        )
+        for j in range(2)
+    )
     real_sq = real * real
     imag_sq = imag * imag
-    level = 0.1 / (half + 1) * jnp.sum(real_sq + imag_sq, axis=1, keepdims=True) + 1e-06
-    inv_real = lax.rsqrt(real_sq + jnp.where(edge, 0.0, imag_sq) + level)
-    inv_imag = jnp.where(edge, lax.rsqrt(imag_sq + level), inv_real)
-    real_ref[...] = (real * inv_real).astype(jnp.bfloat16).astype(jnp.float32)
-    imag_ref[...] = (imag * inv_imag).astype(jnp.bfloat16).astype(jnp.float32)
+    energy = real_sq + imag_sq
+    freqs = real.shape[1] + 1
+    level = 0.1 / freqs * jnp.sum(energy, axis=1, keepdims=True) + 1e-06
+    first, rest = slice(0, LANE), slice(LANE, freqs - 1)
+    edge = lax.broadcasted_iota(jnp.int32, real[:, first].shape, 1) == 0
+    inv_real = lax.rsqrt(jnp.where(edge, real_sq[:, first], energy[:, first]) + level)
+    inv_imag = jnp.where(edge, lax.rsqrt(imag_sq[:, first] + level), inv_real)
+    inverse = lax.rsqrt(energy[:, rest] + level)
+    for ref, value, inv in ((real_ref, real, inv_real), (imag_ref, imag, inv_imag)):
+        for lanes, factor in ((first, inv), (rest, inverse)):
+            whitened = (value[:, lanes] * factor).astype(jnp.bfloat16)
+            ref[:, lanes] = whitened.astype(jnp.float32)
 
 
 def cross_spectra(first, count, chans, segs, left_ref, real_ref, imag_ref, cross):
@@ -206,7 +210,8 @@
 def spectra_scratch(sets, parts, chans, length, share):
     rows, half = sets * parts * SEGS_DEV * chans, length // 2
     return [
-        pltpu.VMEM((rows, 3 * half), jnp.bfloat16),
+        pltpu.VMEM((rows, 3 * length // 4), jnp.bfloat16),
+        pltpu.VMEM((rows, 3 * length // 4), jnp.bfloat16),
         pltpu.VMEM((rows, 3 * half), jnp.bfloat16),
         pltpu.VMEM((rows, half), jnp.float32),
         pltpu.VMEM((rows, half), jnp.float32),
@@ -218,14 +223,16 @@
     return lambda piece, lo, hi: block[piece * chans : (piece + 1) * chans, lo:hi]
 
 
-def correlate_kernel(parts, last_mask, plan, toep, even_table, odd_table, lag_hbm, *refs):
+def correlate_kernel(parts, last_mask, plan_hbm, toep, *refs):
+    fold_tables, lag_hbm, refs = refs[:3], refs[3], refs[4:]
     own, far, near, low, high, refs = *refs[:5], refs[5:]
     far_more, (self_out, pair_out), refs = refs[: parts - 1], refs[parts - 1 : parts + 1], refs[parts + 1 :]
-    lag_table, arrived, far_arrived, left_ref, sums, diffs, real_ref, imag_ref, cross, staged = refs[:10]
-    lag_sem, sems, far_sems, out_sems = refs[10:]
+    plan, lag_table, arrived, far_arrived, left_ref, *refs = refs
+    folds, (real_ref, imag_ref, cross, staged), refs = refs[:3], refs[3:7], refs[7:]
+    plan_sem, lag_sem, sems, far_sems, out_sems = refs
 
     chans, width = far.shape
-    half = even_table.shape[1]
+    half = real_ref.shape[1]
     share = left_ref.shape[0]
     segs = parts * SEGS_DEV
     sets = ROUNDS + 1
@@ -239,7 +246,8 @@
         for i, source in enumerate(far_more)
     ]
     lag_copy = pltpu.make_async_copy(lag_hbm, lag_table, lag_sem)
-    for copy in far_copies + copies + [lag_copy]:
+    plan_copy = pltpu.make_async_copy(plan_hbm, plan, plan_sem)
+    for copy in far_copies + copies + [lag_copy, plan_copy]:
         copy.start()
 
     def far_columns(piece, lo, hi):
@@ -257,8 +265,8 @@
         for copy in needs:
             copy.wait()
         first_row = q * segs * chans
-        add_spectra(columns_of, place, parts, far.shape, first_row, (toep, sums, diffs))
-    whiten(sums, diffs, even_table, odd_table, real_ref, imag_ref)
+        add_spectra(columns_of, place, parts, far.shape, first_row, toep, folds)
+    whiten(folds, fold_tables, real_ref, imag_ref)
 
     def picked(ref, s):
         value = ref[s * chans : s * chans + share, :]
@@ -275,6 +283,7 @@
             for a in range(share):
                 left_ref[a, segs * j + s : segs * j + s + 1, :] = value[a : a + 1]
 
+    plan_copy.wait()
     low_mask, high_mask = free_masks_of(plan, last_mask)
     slots = [
         sum(jnp.where(plan[r] == mask, r, 0) for r in range(ROUNDS))
@@ -319,15 +328,17 @@
             jax.ShapeDtypeStruct((share, chans, LAGS), jnp.float32),
             jax.ShapeDtypeStruct((ROUNDS, share, chans, LAGS), jnp.float32),
         ),
-        in_specs=[SMEM] + [VMEM] * len(table_list) + [HBM] + [VMEM] * 2 + [HBM] * (parts + 2),
+        in_specs=[HBM] + [VMEM] * len(table_list) + [HBM] + [VMEM] * 2 + [HBM] * (parts + 2),
         out_specs=(HBM, HBM),
         scratch_shapes=[
+            pltpu.SMEM(plan.shape, jnp.int32),
             pltpu.VMEM(lag_table.shape, jnp.bfloat16),
             pltpu.VMEM((3, *own.shape), jnp.bfloat16),
             pltpu.VMEM((parts - 1, chans, width), jnp.bfloat16),
             pltpu.VMEM((share, 3 * parts * SEGS_DEV, length // 2), jnp.float32),
             *spectra_scratch(sets, parts, chans, length, share),
             pltpu.VMEM((sets, share, chans, LAGS), jnp.float32),
+            pltpu.SemaphoreType.DMA,
             pltpu.SemaphoreType.DMA,
             pltpu.SemaphoreType.DMA((3,)),
             pltpu.SemaphoreType.DMA((parts - 1,)),

time: 28.5 us -> 32.6 us (1.14)
  waiting for transfers between devices: 7.56 us -> 10.6 us
  starting transfers between devices: 8.71 us -> 10.3 us
  Pallas kernels: 10.6 us -> 9.86 us
    ppermute x4, waiting for transfers between devices: 3.48 us -> 6.48 us  [from_partner(): lax.ppermute(block, 'chan', [(g, g ^ mask) for g in range(chan_count)])]
    ppermute x4, starting transfers between devices: 5.17 us -> 6.74 us  [from_partner(): lax.ppermute(block, 'chan', [(g, g ^ mask) for g in range(chan_count)])]
    pallas_call x1, Pallas kernels: 7.4 us -> 6.88 us  [correlate(): pl.pallas_call(functools.partial(correlate_kernel, parts, last_mask), out...]
  transfers between devices with their start and end apart: 6 -> 6, of which waited for: 2 -> 3; matrix products, arithmetic and copies ran while one was open for 0% -> 0% of each run, Pallas kernels for 11% -> 9%
where the time goes in v1:
time: 32.6 us; the launch traced here: 32.4 us
  waiting for transfers between devices  10.6 us (33%)
  starting transfers between devices  10.3 us (32%)
  Pallas kernels  9.86 us (30%)
  between operations  1.49 us (5%)
    pallas_call x1, Pallas kernels, correlate(): pl.pallas_call(functools.partial(correlate_kernel, parts, last_mask), out...  6.88 us
    ppermute x4, starting transfers between devices, from_partner(): lax.ppermute(block, 'chan', [(g, g ^ mask) for g in range(chan_count)])  6.74 us
    ppermute x4, waiting for transfers between devices, from_partner(): lax.ppermute(block, 'chan', [(g, g ^ mask) for g in range(chan_count)])  6.48 us
    ppermute x2, waiting for transfers between devices, from_times(): lax.ppermute(block, 'tm', [(t, (t + j) % parts) for t in range(parts)])  4.08 us
    ppermute x2, starting transfers between devices, from_times(): lax.ppermute(block, 'tm', [(t, (t + j) % parts) for t in range(parts)])  3.54 us
    pallas_call x1, Pallas kernels, prepare(): pl.pallas_call(functools.partial(prepare_kernel, last_mask), out_shape=(j...  2.98 us
  transfers between devices with their start and end apart: 6, of which 3 were waited for; matrix products, arithmetic and copies ran while one was open for 0% of the time, Pallas kernels for 9%

profile of v1, /device:TPU:0, one launch (start us, length us, event | category | flops | bytes accessed | tf_op | source)
XLA Modules:
  0.0 32.4 jit_solution(15998561519298553869)
XLA Ops:
  0.6 3.0 %collective-permute-start.312 = (bf16[16,2048]{1,0:T(8,128)(2,1)}, bf16[16,2048]{1,0:T(8,128)(2,1)S(1)}, u32[]{:S(2)}, u32[]{:S(2)}) collective-permute-start(bf16[16,2048]{1,0:T(8,128)(2,1)} %samples.1), channel_id=1, source_target_pairs={{0,1},{1,0},{2,3},{3,2},{4,5},{5,4},{6,7},{7,6},{8,9},{9,8},{10,11... | collective-permute-start | bytes 196616 | tf_op jit(solution)/shard_map/ppermute | solution.py:359
  3.6 3.7 %collective-permute-start.313 = (bf16[16,2048]{1,0:T(8,128)(2,1)}, bf16[16,2048]{1,0:T(8,128)(2,1)S(1)}, u32[]{:S(2)}, u32[]{:S(2)}) collective-permute-start(bf16[16,2048]{1,0:T(8,128)(2,1)} %samples.1), channel_id=1, source_target_pairs={{0,30},{2,28},{4,26},{6,24},{8,22},{10,20},{12,18},{14,16},{16,14}... | collective-permute-start | bytes 196616 | tf_op jit(solution)/shard_map/ppermute | solution.py:353
  7.4 3.0 %shard_map.86 = (s32[1]{0:T(128)}, bf16[32,2048]{1,0:T(8,128)(2,1)S(1)}, bf16[256,256]{1,0:T(8,128)(2,1)S(1)}, bf16[768,256]{1,0:T(8,128)(2,1)S(1)}, bf16[768,25...) custom-call(s32[4]{0:T(128)} %plan_hbm.1, f32[96]{0:T(128)} %taps.1, bf16[16,2048]{1,0:T(8,128)(2,1)} %samples.1, ...), custom_call_target="tpu_custom_call" | custom-call | tf_op jit(solution)/shard_map/pallas_call | solution.py:105
  11.0 0.0 collective-permute-done.312
  11.0 0.0 collective-permute-done.313.refs_5_
  11.0 14.3 %conditional.1 = (bf16[32,2048]{1,0:T(8,128)(2,1)}, bf16[16,2048]{1,0:T(8,128)(2,1)}, bf16[32,2048]{1,0:T(8,128)(2,1)}, bf16[32,2048]{1,0:T(8,128)(2,1)}) conditional(s32[]{:T(128)} %bitcast, (bf16[32,2048]{1,0:T(8,128)(2,1)S(1)}, bf16[16,2048]{1,0:T(8,128)(2,1)S(1)}) %tuple.319, (bf16[32,2048]{1,0:T(8,128)(2,1)S(1)}, ...), branch_computations={%region_0.0_spmd, %region_1.0_spmd, %region_2.0_spmd, %region_3.0_... | conditional | bytes 1835200 | solution.py:382
  11.3 3.0 %collective-permute-start.211 = (bf16[32,2048]{1,0:T(8,128)(2,1)S(1)}, bf16[32,2048]{1,0:T(8,128)(2,1)}, u32[]{:S(2)}, u32[]{:S(2)}) collective-permute-start(bf16[32,2048]{1,0:T(8,128)(2,1)S(1)} %get-tuple-element.416), channel_id=1, source_target_pairs={{0,24},{2,26},{4,28},{6,30},{8,16},{10,18},{12,20},{14,22},{16,8},... | collective-permute-start | bytes 393224 | tf_op jit(solution)/shard_map/cond/branch_52_fun/ppermute | solution.py:353
  14.3 0.0 collective-permute-start.210
  14.3 0.0 collective-permute-start.208
  14.3 0.5 %collective-permute-start.209 = (bf16[16,2048]{1,0:T(8,128)(2,1)S(1)}, bf16[16,2048]{1,0:T(8,128)(2,1)}, u32[]{:S(2)}, u32[]{:S(2)}) collective-permute-start(bf16[16,2048]{1,0:T(8,128)(2,1)S(1)} %get-tuple-element.417), channel_id=1, source_target_pairs={{0,1},{1,0},{2,3},{3,2},{4,5},{5,4},{6,7},{7,6},{8,9},{9,8},{10,11... | collective-permute-start | bytes 196616 | tf_op jit(solution)/shard_map/cond/branch_52_fun/ppermute | solution.py:359
  14.8 4.1 %collective-permute-done.209 = bf16[16,2048]{1,0:T(8,128)(2,1)} collective-permute-done((bf16[16,2048]{1,0:T(8,128)(2,1)S(1)}, bf16[16,2048]{1,0:T(8,128)(2,1)}, u32[]{:S(2)}, u32[]{:S(2)}) %collective-permute-start.209) | collective-permute-done | bytes 65568 | tf_op jit(solution)/shard_map/cond/branch_52_fun/ppermute | solution.py:359
  18.9 0.8 %collective-permute-done.211 = bf16[32,2048]{1,0:T(8,128)(2,1)} collective-permute-done((bf16[32,2048]{1,0:T(8,128)(2,1)S(1)}, bf16[32,2048]{1,0:T(8,128)(2,1)}, u32[]{:S(2)}, u32[]{:S(2)}) %collective-permute-start.211) | collective-permute-done | bytes 131104 | tf_op jit(solution)/shard_map/cond/branch_52_fun/ppermute | solution.py:353
  19.7 5.7 %collective-permute-done.210 = bf16[32,2048]{1,0:T(8,128)(2,1)} collective-permute-done((bf16[32,2048]{1,0:T(8,128)(2,1)S(1)}, bf16[32,2048]{1,0:T(8,128)(2,1)}, u32[]{:S(2)}, u32[]{:S(2)}) %collective-permute-start.210) | collective-permute-done | bytes 131104 | tf_op jit(solution)/shard_map/cond/branch_52_fun/ppermute | solution.py:353
  25.4 0.0 collective-permute-done.208
  25.4 6.9 %shard_map.87 = (f32[8,16,129]{2,1,0:T(8,128)}, f32[4,8,16,129]{3,2,1,0:T(8,128)}) custom-call(s32[4]{0:T(128)} %plan_hbm.1, bf16[256,256]{1,0:T(8,128)(2,1)S(1)} %get-tuple-element.480.toep, bf16[768,256]{1,0:T(8,128)(2,1)S(1)} %get-tuple-element.481.refs_0_, bf16[768,256]{1,0:T(8,128)(2,1)S(1)} %get-tuple-element.482.refs_1_, ...), custom_call_target="tpu_custom_call" | custom-call | tf_op jit(solution)/shard_map/pallas_call | solution.py:325
  (1 shorter events, 0.0 us)
Async XLA Ops:
  0.6 10.4 %collective-permute-start.312 = (bf16[16,2048]{1,0:T(8,128)(2,1)}, bf16[16,2048]{1,0:T(8,128)(2,1)S(1)}, u32[]{:S(2)}, u32[]{:S(2)}) collective-permute-start(bf16[16,2048]{1,0:T(8,128)(2,1)} %samples.1), channel_id=1, source_target_pairs={{0,1},{1,0},{2,3},{3,2},{4,5},{5,4},{6,7},{7,6},{8,9},{9,8},{10,11... | collective-permute-start | bytes 196616 | tf_op jit(solution)/shard_map/ppermute | solution.py:359
  3.6 7.4 %collective-permute-start.313 = (bf16[16,2048]{1,0:T(8,128)(2,1)}, bf16[16,2048]{1,0:T(8,128)(2,1)S(1)}, u32[]{:S(2)}, u32[]{:S(2)}) collective-permute-start(bf16[16,2048]{1,0:T(8,128)(2,1)} %samples.1), channel_id=1, source_target_pairs={{0,30},{2,28},{4,26},{6,24},{8,22},{10,20},{12,18},{14,16},{16,14}... | collective-permute-start | bytes 196616 | tf_op jit(solution)/shard_map/ppermute | solution.py:353
  11.3 8.4 %collective-permute-start.211 = (bf16[32,2048]{1,0:T(8,128)(2,1)S(1)}, bf16[32,2048]{1,0:T(8,128)(2,1)}, u32[]{:S(2)}, u32[]{:S(2)}) collective-permute-start(bf16[32,2048]{1,0:T(8,128)(2,1)S(1)} %get-tuple-element.416), channel_id=1, source_target_pairs={{0,24},{2,26},{4,28},{6,30},{8,16},{10,18},{12,20},{14,22},{16,8},... | collective-permute-start | bytes 393224 | tf_op jit(solution)/shard_map/cond/branch_52_fun/ppermute | solution.py:353
  14.3 11.1 %collective-permute-start.210 = (bf16[32,2048]{1,0:T(8,128)(2,1)S(1)}, bf16[32,2048]{1,0:T(8,128)(2,1)}, u32[]{:S(2)}, u32[]{:S(2)}) collective-permute-start(bf16[32,2048]{1,0:T(8,128)(2,1)S(1)} %get-tuple-element.416), channel_id=1, source_target_pairs={{0,18},{2,16},{4,22},{6,20},{8,26},{10,24},{12,30},{14,28},{16,2},... | collective-permute-start | bytes 393224 | tf_op jit(solution)/shard_map/cond/branch_52_fun/ppermute | solution.py:353
  14.3 11.1 %collective-permute-start.208 = (bf16[32,2048]{1,0:T(8,128)(2,1)S(1)}, bf16[32,2048]{1,0:T(8,128)(2,1)}, u32[]{:S(2)}, u32[]{:S(2)}) collective-permute-start(bf16[32,2048]{1,0:T(8,128)(2,1)S(1)} %get-tuple-element.416), channel_id=1, source_target_pairs={{0,2},{2,0},{4,6},{6,4},{8,10},{10,8},{12,14},{14,12},{16,18},{18,... | collective-permute-start | bytes 393224 | tf_op jit(solution)/shard_map/cond/branch_52_fun/ppermute | solution.py:353
  14.3 4.6 %collective-permute-start.209 = (bf16[16,2048]{1,0:T(8,128)(2,1)S(1)}, bf16[16,2048]{1,0:T(8,128)(2,1)}, u32[]{:S(2)}, u32[]{:S(2)}) collective-permute-start(bf16[16,2048]{1,0:T(8,128)(2,1)S(1)} %get-tuple-element.417), channel_id=1, source_target_pairs={{0,1},{1,0},{2,3},{3,2},{4,5},{5,4},{6,7},{7,6},{8,9},{9,8},{10,11... | collective-permute-start | bytes 196616 | tf_op jit(solution)/shard_map/cond/branch_52_fun/ppermute | solution.py:359
